TPU v7x, 32 devices: a whole 2x2x4 slice. The times are simulated.
32 devices in a mesh: rows: 8 (over z, x), rhs: 4 (over y, core).
Axes of the slice: x: 2, y: 2, z: 4, core: 2. Of those that a mesh axis runs over, the one named last changes fastest.
Arguments:
- start: bfloat16 [128, 16384], P('rhs', 'rows')
- tiles: bfloat16 [128, 12, 128, 128], P('rows'), may hold values from -0.21875 to 0.21875
- cols: int32 [128, 12], P('rows'), may hold values from 0 to 127, as said below
- counts: int32 [128], P('rows'), may hold values from 3 to 12
Outputs:
- basis: bfloat16 [4, 128, 16384], P(None, 'rhs', 'rows')
- gram: float32 [4, 160, 160], P('rhs')
Inputs may be any that keep to these rules, and one draw needn't show every extreme that they name: cols[b, t] names a row block held by the same index of rows as b or by the index on either side of it: b // 16 - 1 <= cols[b, t] // 16 <= b // 16 + 1.
All inputs are finite; a program needn't handle non-finite values.
Results may differ from a plain program's by a relative error of at most 0.015.
Values sent between devices are 32-bit elements; how exact they have to be, the bound alone decides.
A program may use at most 64 MiB of HBM per device.

v0:
```python
import jax
import jax.numpy as jnp
from jax import lax
from jax.sharding import PartitionSpec as P

S = 4


def shifted(block, axis, distance):
    devices = range(lax.axis_size(axis))
    route = [(i - distance, i) for i in devices if i - distance in devices]
    return lax.ppermute(block, axis, route)


def place_sum(onehot, contrib):
    high = contrib.astype(jnp.bfloat16)
    remainder = (contrib - high.astype(jnp.float32)).astype(jnp.bfloat16)
    upper = jnp.einsum("sb,spj->pbj", onehot, high, preferred_element_type=jnp.float32)
    lower = jnp.einsum("sb,spj->pbj", onehot, remainder, preferred_element_type=jnp.float32)
    return upper + lower


def padded_apply(vector, tiles, cols, counts, first):
    panel, rows_dev = vector.shape
    blocks, slots, blk, _ = tiles.shape
    blocked = vector.reshape(panel, blocks, blk)
    contrib = jnp.einsum("pri,rtij->rtpj", blocked, tiles, preferred_element_type=jnp.float32)
    contrib = contrib.reshape(blocks * slots, panel, blk)
    used = jnp.arange(slots, dtype=jnp.int32)[None, :] < counts[:, None]
    target = (cols - first).reshape(-1)
    onehot = (target[:, None] == jnp.arange(3 * blocks, dtype=jnp.int32)[None, :]) & used.reshape(
        -1
    )[:, None]
    onehot = onehot.astype(jnp.bfloat16)
    total = place_sum(onehot, contrib)
    return total.reshape(panel, 3 * rows_dev)


def body(start, tiles, cols, counts):
    panel, rows_dev = start.shape
    blocks = tiles.shape[0]
    first = (lax.axis_index("rows") - 1) * blocks
    vector = start
    powers = []
    for power in range(S):
        partial_value = padded_apply(vector, tiles, cols, counts, first)
        to_prev = partial_value[:, :rows_dev]
        own = partial_value[:, rows_dev : 2 * rows_dev]
        to_next = partial_value[:, 2 * rows_dev :]
        from_prev = shifted(to_next, "rows", 1)
        from_next = shifted(to_prev, "rows", -1)
        summed = own + from_prev + from_next
        vector = summed.astype(jnp.bfloat16)
        powers.append(vector)
    basis = jnp.stack(powers)
    stacked = jnp.concatenate([start[None], basis], axis=0)
    total_rows = rows_dev * lax.axis_size("rows")
    flat = stacked.reshape((S + 1) * panel, rows_dev)
    local_gram = lax.dot_general(
        flat, flat, (((1,), (1,)), ((), ())), preferred_element_type=jnp.float32
    )
    gram = lax.psum(local_gram, "rows")
    return (basis, (gram / total_rows)[None])


def solution(mesh):
    return jax.shard_map(
        body,
        mesh=mesh,
        in_specs=(P("rhs", "rows"), P("rows", None, None, None), P("rows", None), P("rows")),
        out_specs=(P(None, "rhs", "rows"), P("rhs", None, None)),
        check_vma=False,
    )
```

profile of v0, /device:TPU:0, one launch (start us, length us, event | category | flops | bytes accessed | tf_op | source)
XLA Modules:
  0.0 180.0 jit_solution(14506525776682271221)
XLA Ops:
  7.2 0.0 all-reduce.2.cloned.1.call-start
  7.2 0.7 iota_compare_fusion.1
  7.9 0.1 lt.16
  8.0 0.7 broadcast_subtract_fusion
  8.7 0.1 eq.8
  8.8 0.9 copy.30
  9.8 0.0 slice-start
  9.8 0.0 slice-start.1
  9.8 3.9 %fusion.27 = f32[16,12,128,32]{2,3,1,0:T(8,128)S(1)} fusion(bf16[16,12,128,128]{3,2,1,0:T(8,128)(2,1)} %param.5, bf16[32,16,128,1]{2,1,0,3:T(8,128)(2,1)S(1)} %bitcast.107), kind=kOutput, calls=%fused_computation.46 | convolution fusion | flops 201326592 | bytes 9568256 | tf_op jit(solution)/shard_map/pri,rtij->rtpj/dot_general | solution.py:27
  13.7 1.8 %fusion = f32[32,128,48]{1,2,0:T(8,128)S(1)} fusion(f32[192,32,128]{2,1,0:T(8,128)S(1)} %bitcast.82, s32[192]{0:T(256)S(1)} %eq.8, pred[192]{0:T(512)(128)(4,1)S(1)} %lt.16), kind=kOutput, calls=%fused_computation.8 | convolution fusion | flops 75515904 | bytes 3933120 | tf_op jit(solution)/shard_map/sb,spj->pbj/dot_general | solution.py:18
  15.5 0.0 copy-start
  15.5 1.8 %fusion.11 = f32[32,128,48]{1,2,0:T(8,128)S(1)} fusion(f32[32,128,48]{1,2,0:T(8,128)S(1)} %fusion, f32[192,32,128]{2,1,0:T(8,128)S(1)} %bitcast.83, s32[192]{0:T(256)S(1)} %eq.8, pred[192]{0:T(512)(128)(4,1)S(1)} %lt.16), kind=kOutput, calls=%fused_computation.19 | convolution fusion | flops 78858240 | bytes 4719552 | tf_op jit(solution)/shard_map/sb,spj->pbj/dot_general | solution.py:19
  17.4 0.2 copy.85
  17.7 4.9 %collective-permute-start = (f32[32,2048]{1,0:T(8,128)S(1)}, f32[32,2048]{1,0:T(8,128)S(1)}, u32[]{:S(2)}, u32[]{:S(2)}) collective-permute-start(f32[32,2048]{1,0:T(8,128)S(1)} %get-tuple-element.16), channel_id=1, source_target_pairs={{0,4},{4,8},{8,12},{12,16},{16,20},{20,24},{24,28},{1,5},{5,9},{9,... | collective-permute-start | bytes 786440 | tf_op jit(solution)/shard_map/ppermute | solution.py:12
  22.5 1.3 collective-permute-start.1
  23.8 0.0 copy-done
  23.9 9.8 %collective-permute-done = f32[32,2048]{1,0:T(8,128)S(1)} collective-permute-done((f32[32,2048]{1,0:T(8,128)S(1)}, f32[32,2048]{1,0:T(8,128)S(1)}, u32[]{:S(2)}, u32[]{:S(2)}) %collective-permute-start) | collective-permute-done | bytes 262176 | tf_op jit(solution)/shard_map/ppermute | solution.py:12
  33.7 0.0 collective-permute-done.1
  33.8 0.0 slice-done
  33.8 0.0 slice-done.1
  33.8 1.0 fusion.25
  34.8 1.8 %fusion.1 = f32[32,128,48]{1,2,0:T(8,128)S(1)} fusion(f32[192,32,128]{2,1,0:T(8,128)S(1)} %bitcast.84, s32[192]{0:T(256)S(1)} %eq.8, pred[192]{0:T(512)(128)(4,1)S(1)} %lt.16), kind=kOutput, calls=%fused_computation.9 | convolution fusion | flops 75515904 | bytes 3933120 | tf_op jit(solution)/shard_map/sb,spj->pbj/dot_general | solution.py:18
  36.6 1.8 %fusion.10 = f32[32,128,48]{1,2,0:T(8,128)S(1)} fusion(f32[32,128,48]{1,2,0:T(8,128)S(1)} %fusion.1, f32[192,32,128]{2,1,0:T(8,128)S(1)} %bitcast.85, s32[192]{0:T(256)S(1)} %eq.8, pred[192]{0:T(512)(128)(4,1)S(1)} %lt.16), kind=kOutput, calls=%fused_computation.18 | convolution fusion | flops 78858240 | bytes 4719552 | tf_op jit(solution)/shard_map/sb,spj->pbj/dot_general | solution.py:19
  38.4 0.2 copy.84
  38.7 4.4 %collective-permute-start.2 = (f32[32,2048]{1,0:T(8,128)S(1)}, f32[32,2048]{1,0:T(8,128)S(1)}, u32[]{:S(2)}, u32[]{:S(2)}) collective-permute-start(f32[32,2048]{1,0:T(8,128)S(1)} %get-tuple-element.14), channel_id=1, source_target_pairs={{0,4},{4,8},{8,12},{12,16},{16,20},{20,24},{24,28},{1,5},{5,9},{9,... | collective-permute-start | bytes 786440 | tf_op jit(solution)/shard_map/ppermute | solution.py:12
  43.1 1.5 collective-permute-start.3
  44.6 3.2 %collective-permute-done.2 = f32[32,2048]{1,0:T(8,128)S(1)} collective-permute-done((f32[32,2048]{1,0:T(8,128)S(1)}, f32[32,2048]{1,0:T(8,128)S(1)}, u32[]{:S(2)}, u32[]{:S(2)}) %collective-permute-start.2) | collective-permute-done | bytes 262176 | tf_op jit(solution)/shard_map/ppermute | solution.py:12
  47.8 5.9 %collective-permute-done.3 = f32[32,2048]{1,0:T(8,128)S(1)} collective-permute-done((f32[32,2048]{1,0:T(8,128)S(1)}, f32[32,2048]{1,0:T(8,128)S(1)}, u32[]{:S(2)}, u32[]{:S(2)}) %collective-permute-start.3) | collective-permute-done | bytes 262176 | tf_op jit(solution)/shard_map/ppermute | solution.py:12
  53.8 1.0 fusion.23
  54.7 1.8 %fusion.2 = f32[32,128,48]{1,2,0:T(8,128)S(1)} fusion(f32[192,32,128]{2,1,0:T(8,128)S(1)} %bitcast.86, s32[192]{0:T(256)S(1)} %eq.8, pred[192]{0:T(512)(128)(4,1)S(1)} %lt.16), kind=kOutput, calls=%fused_computation.10 | convolution fusion | flops 75515904 | bytes 3933120 | tf_op jit(solution)/shard_map/sb,spj->pbj/dot_general | solution.py:18
  56.6 1.8 %fusion.9 = f32[32,128,48]{1,2,0:T(8,128)S(1)} fusion(f32[32,128,48]{1,2,0:T(8,128)S(1)} %fusion.2, f32[192,32,128]{2,1,0:T(8,128)S(1)} %bitcast.87, s32[192]{0:T(256)S(1)} %eq.8, pred[192]{0:T(512)(128)(4,1)S(1)} %lt.16), kind=kOutput, calls=%fused_computation.17 | convolution fusion | flops 78858240 | bytes 4719552 | tf_op jit(solution)/shard_map/sb,spj->pbj/dot_general | solution.py:19
  58.4 0.2 copy.83
  58.7 4.5 %collective-permute-start.4 = (f32[32,2048]{1,0:T(8,128)S(1)}, f32[32,2048]{1,0:T(8,128)S(1)}, u32[]{:S(2)}, u32[]{:S(2)}) collective-permute-start(f32[32,2048]{1,0:T(8,128)S(1)} %get-tuple-element.12), channel_id=1, source_target_pairs={{0,4},{4,8},{8,12},{12,16},{16,20},{20,24},{24,28},{1,5},{5,9},{9,... | collective-permute-start | bytes 786440 | tf_op jit(solution)/shard_map/ppermute | solution.py:12
  63.3 1.3 collective-permute-start.5
  64.6 3.2 %collective-permute-done.4 = f32[32,2048]{1,0:T(8,128)S(1)} collective-permute-done((f32[32,2048]{1,0:T(8,128)S(1)}, f32[32,2048]{1,0:T(8,128)S(1)}, u32[]{:S(2)}, u32[]{:S(2)}) %collective-permute-start.4) | collective-permute-done | bytes 262176 | tf_op jit(solution)/shard_map/ppermute | solution.py:12
  67.8 7.5 %collective-permute-done.5 = f32[32,2048]{1,0:T(8,128)S(1)} collective-permute-done((f32[32,2048]{1,0:T(8,128)S(1)}, f32[32,2048]{1,0:T(8,128)S(1)}, u32[]{:S(2)}, u32[]{:S(2)}) %collective-permute-start.5) | collective-permute-done | bytes 262176 | tf_op jit(solution)/shard_map/ppermute | solution.py:12
  75.4 0.9 fusion.21
  76.4 1.8 %fusion.3 = f32[32,128,48]{1,2,0:T(8,128)S(1)} fusion(f32[192,32,128]{2,1,0:T(8,128)S(1)} %bitcast.80, s32[192]{0:T(256)S(1)} %eq.8, pred[192]{0:T(512)(128)(4,1)S(1)} %lt.16), kind=kOutput, calls=%fused_computation.11 | convolution fusion | flops 75515904 | bytes 3933120 | tf_op jit(solution)/shard_map/sb,spj->pbj/dot_general | solution.py:18
  78.2 1.8 %fusion.8 = f32[32,128,48]{1,2,0:T(8,128)S(1)} fusion(f32[32,128,48]{1,2,0:T(8,128)S(1)} %fusion.3, f32[192,32,128]{2,1,0:T(8,128)S(1)} %bitcast.81, s32[192]{0:T(256)S(1)} %eq.8, pred[192]{0:T(512)(128)(4,1)S(1)} %lt.16), kind=kOutput, calls=%fused_computation.16 | convolution fusion | flops 78858240 | bytes 4719552 | tf_op jit(solution)/shard_map/sb,spj->pbj/dot_general | solution.py:19
  80.1 0.2 copy.82
  80.4 4.6 %collective-permute-start.6 = (f32[32,2048]{1,0:T(8,128)S(1)}, f32[32,2048]{1,0:T(8,128)S(1)}, u32[]{:S(2)}, u32[]{:S(2)}) collective-permute-start(f32[32,2048]{1,0:T(8,128)S(1)} %get-tuple-element.10), channel_id=1, source_target_pairs={{0,4},{4,8},{8,12},{12,16},{16,20},{20,24},{24,28},{1,5},{5,9},{9,... | collective-permute-start | bytes 786440 | tf_op jit(solution)/shard_map/ppermute | solution.py:12
  84.9 1.3 collective-permute-start.7
  86.2 3.3 %collective-permute-done.6 = f32[32,2048]{1,0:T(8,128)S(1)} collective-permute-done((f32[32,2048]{1,0:T(8,128)S(1)}, f32[32,2048]{1,0:T(8,128)S(1)}, u32[]{:S(2)}, u32[]{:S(2)}) %collective-permute-start.6) | collective-permute-done | bytes 262176 | tf_op jit(solution)/shard_map/ppermute | solution.py:12
  89.5 7.5 %collective-permute-done.7 = f32[32,2048]{1,0:T(8,128)S(1)} collective-permute-done((f32[32,2048]{1,0:T(8,128)S(1)}, f32[32,2048]{1,0:T(8,128)S(1)}, u32[]{:S(2)}, u32[]{:S(2)}) %collective-permute-start.7) | collective-permute-done | bytes 262176 | tf_op jit(solution)/shard_map/ppermute | solution.py:12
  97.1 1.0 fusion.47
  98.1 0.0 all-reduce.2.cloned.1.call-update
  98.1 0.9 pad_maximum_fusion
  98.9 72.6 %all-reduce.2.cloned.1.call-done = f32[160,160]{1,0:T(8,128)} async-done(((f32[160,160]{1,0:T(8,128)}), f32[160,160]{1,0:T(8,128)}) %all-reduce.2.cloned.1.call-update) | async-done | bytes 102416 | tf_op jit(solution)/shard_map/psum | solution.py:62
  171.5 1.6 multiply_bitcast_fusion
  (13 shorter events, 0.4 us)
Async XLA Ops:
  7.2 164.4 %all-reduce.2.cloned.1.call-start = ((), (), s32[]{:S(2)}) async-start(), calls=%async_computation | async-start | bytes 327680 | tf_op jit(solution)/shard_map/psum | solution.py:62
  9.8 24.0 %slice-start = ((s8[6291456]{0:T(1024)(128)(4,1)}), s8[4194304]{0:T(1024)(128)(4,1)S(1)}, s32[]{:S(2)}) async-start(s8[6291456]{0:T(1024)(128)(4,1)} %bitcast.78), calls=%async_computation.1 | async-start | bytes 8388608
  9.8 24.0 %slice-start.1 = ((s8[6291456]{0:T(1024)(128)(4,1)}), s8[2097152]{0:T(1024)(128)(4,1)S(1)}, s32[]{:S(2)}) async-start(s8[6291456]{0:T(1024)(128)(4,1)} %bitcast.78), calls=%async_computation.2 | async-start | bytes 4194304
  15.5 8.3 %copy-start = (bf16[32,2048]{1,0:T(8,128)(2,1)S(1)}, bf16[32,2048]{1,0:T(8,128)(2,1)}, u32[]{:S(2)}) copy-start(bf16[32,2048]{1,0:T(8,128)(2,1)} %param.4) | copy-start | bytes 393220
  17.7 16.0 %collective-permute-start = (f32[32,2048]{1,0:T(8,128)S(1)}, f32[32,2048]{1,0:T(8,128)S(1)}, u32[]{:S(2)}, u32[]{:S(2)}) collective-permute-start(f32[32,2048]{1,0:T(8,128)S(1)} %get-tuple-element.16), channel_id=1, source_target_pairs={{0,4},{4,8},{8,12},{12,16},{16,20},{20,24},{24,28},{1,5},{5,9},{9,... | collective-permute-start | bytes 786440 | tf_op jit(solution)/shard_map/ppermute | solution.py:12
  22.5 11.2 %collective-permute-start.1 = (f32[32,2048]{1,0:T(8,128)S(1)}, f32[32,2048]{1,0:T(8,128)S(1)}, u32[]{:S(2)}, u32[]{:S(2)}) collective-permute-start(f32[32,2048]{1,0:T(8,128)S(1)} %get-tuple-element.17), channel_id=1, source_target_pairs={{4,0},{8,4},{12,8},{16,12},{20,16},{24,20},{28,24},{5,1},{9,5},{13... | collective-permute-start | bytes 786440 | tf_op jit(solution)/shard_map/ppermute | solution.py:12
  38.7 9.1 %collective-permute-start.2 = (f32[32,2048]{1,0:T(8,128)S(1)}, f32[32,2048]{1,0:T(8,128)S(1)}, u32[]{:S(2)}, u32[]{:S(2)}) collective-permute-start(f32[32,2048]{1,0:T(8,128)S(1)} %get-tuple-element.14), channel_id=1, source_target_pairs={{0,4},{4,8},{8,12},{12,16},{16,20},{20,24},{24,28},{1,5},{5,9},{9,... | collective-permute-start | bytes 786440 | tf_op jit(solution)/shard_map/ppermute | solution.py:12
  43.1 10.5 %collective-permute-start.3 = (f32[32,2048]{1,0:T(8,128)S(1)}, f32[32,2048]{1,0:T(8,128)S(1)}, u32[]{:S(2)}, u32[]{:S(2)}) collective-permute-start(f32[32,2048]{1,0:T(8,128)S(1)} %get-tuple-element.15), channel_id=1, source_target_pairs={{4,0},{8,4},{12,8},{16,12},{20,16},{24,20},{28,24},{5,1},{9,5},{13... | collective-permute-start | bytes 786440 | tf_op jit(solution)/shard_map/ppermute | solution.py:12
  58.7 9.1 %collective-permute-start.4 = (f32[32,2048]{1,0:T(8,128)S(1)}, f32[32,2048]{1,0:T(8,128)S(1)}, u32[]{:S(2)}, u32[]{:S(2)}) collective-permute-start(f32[32,2048]{1,0:T(8,128)S(1)} %get-tuple-element.12), channel_id=1, source_target_pairs={{0,4},{4,8},{8,12},{12,16},{16,20},{20,24},{24,28},{1,5},{5,9},{9,... | collective-permute-start | bytes 786440 | tf_op jit(solution)/shard_map/ppermute | solution.py:12
  63.3 12.1 %collective-permute-start.5 = (f32[32,2048]{1,0:T(8,128)S(1)}, f32[32,2048]{1,0:T(8,128)S(1)}, u32[]{:S(2)}, u32[]{:S(2)}) collective-permute-start(f32[32,2048]{1,0:T(8,128)S(1)} %get-tuple-element.13), channel_id=1, source_target_pairs={{4,0},{8,4},{12,8},{16,12},{20,16},{24,20},{28,24},{5,1},{9,5},{13... | collective-permute-start | bytes 786440 | tf_op jit(solution)/shard_map/ppermute | solution.py:12
  80.4 9.1 %collective-permute-start.6 = (f32[32,2048]{1,0:T(8,128)S(1)}, f32[32,2048]{1,0:T(8,128)S(1)}, u32[]{:S(2)}, u32[]{:S(2)}) collective-permute-start(f32[32,2048]{1,0:T(8,128)S(1)} %get-tuple-element.10), channel_id=1, source_target_pairs={{0,4},{4,8},{8,12},{12,16},{16,20},{20,24},{24,28},{1,5},{5,9},{9,... | collective-permute-start | bytes 786440 | tf_op jit(solution)/shard_map/ppermute | solution.py:12
  84.9 12.1 %collective-permute-start.7 = (f32[32,2048]{1,0:T(8,128)S(1)}, f32[32,2048]{1,0:T(8,128)S(1)}, u32[]{:S(2)}, u32[]{:S(2)}) collective-permute-start(f32[32,2048]{1,0:T(8,128)S(1)} %get-tuple-element.11), channel_id=1, source_target_pairs={{4,0},{8,4},{12,8},{16,12},{20,16},{24,20},{28,24},{5,1},{9,5},{13... | collective-permute-start | bytes 786440 | tf_op jit(solution)/shard_map/ppermute | solution.py:12
Sparse Core Ops, SparseCore 0:
  98.2 73.2 all-reduce.1
where the time goes:
time: 180 us
  waiting for transfers between devices  113 us (63%)
  starting transfers between devices  23.8 us (13%)
  matrix products  22.5 us (12%)
  between operations  14.3 us (8%)
  other arithmetic  4.06 us (2%)
  local copies, waits for them, and re-layouts  2.32 us (1%)
    psum x1, waiting for transfers between devices, body(): gram = lax.psum(local_gram, 'rows')  72.6 us
    ppermute x8, waiting for transfers between devices, shifted(): return lax.ppermute(block, axis, route)  40.4 us
    ppermute x8, starting transfers between devices, shifted(): return lax.ppermute(block, axis, route)  23.7 us
    dot_general x4, matrix products, place_sum(): jnp.einsum('sb,spj->pbj', onehot, remainder, preferred_element_type=jnp.f...  7.39 us
    dot_general x4, matrix products, place_sum(): jnp.einsum('sb,spj->pbj', onehot, high, preferred_element_type=jnp.float32)  7.32 us
    dot_general x4, matrix products, padded_apply(): jnp.einsum('pri,rtij->rtpj', blocked, tiles, preferred_element_type=jnp.f...  6.74 us
  transfers between devices with their start and end apart: 9, of which 8 were waited for; matrix products, arithmetic and copies ran while one was open for 0% of the time, Pallas kernels for 0%

commit v1 on v0

v1 whole, which is shorter than its diff:
```python
import functools

import jax
import jax.numpy as jnp
from jax import lax
from jax.experimental import pallas as pl
from jax.experimental.pallas import tpu as pltpu
from jax.sharding import PartitionSpec as P

S = 4
HALVES = 2
CHUNKS = 2
UNROLL = 16
MESH = pl.DeviceIdType.MESH


def schedule(cols, counts, devices):
    blocks, slots = cols.shape
    total = blocks * slots
    r = lax.axis_index("rows")
    rel = cols - (r - 1) * blocks
    side = rel // blocks
    even = r % 2 == 0
    group = jnp.where(side == 1, 2, jnp.where((side == 0) == even, 0, 1))
    target = group * blocks + rel % blocks
    used = jnp.arange(slots, dtype=jnp.int32)[None, :] < counts[:, None]
    target = jnp.where(used, target, 3 * blocks).reshape(-1)
    item = jnp.arange(total, dtype=jnp.int32)
    earlier = target[None, :] < target[:, None]
    tied = (target[None, :] == target[:, None]) & (item[None, :] < item[:, None])
    rank = jnp.sum(earlier | tied, axis=1, dtype=jnp.int32)
    opens = jnp.logical_not(jnp.any(tied, axis=1)).astype(jnp.int32)
    code = ((item // slots) * total + item) * 2 + opens
    placed = jnp.sum(jnp.where(rank[None, :] == item[:, None], code[None, :], 0), axis=1, dtype=jnp.int32)
    c = jnp.arange(3 * blocks, dtype=jnp.int32)[:, None]
    upto = jnp.sum(target[None, :] <= c, axis=1, dtype=jnp.int32)
    here = jnp.any(target[None, :] == c, axis=1)
    last = jnp.where(here, upto - 1, total)
    return jnp.concatenate([placed, last])


def kernel(
    n, blocks, slots, start_ref, tiles_hbm, code_ref, basis_ref, gram_ref,
    tiles, x, sums0, sums1, far_out, far_in, near_out, near_in,
    early, early_in, late, late_in,
    tile_sem, far_send, far_recv, near_send, near_recv, gram_send, gram_recv,
):
    total = blocks * slots
    sums = (sums0, sums1)
    rows = start_ref.shape[0] // HALVES
    blk = tiles.shape[-1]
    per = blocks // CHUNKS
    stages = n.bit_length() - 1
    r = lax.axis_index("rows")
    parity = r % 2
    step = 4 * parity - 2
    to, frm = r + step, r - step
    sends_far = jnp.logical_and(to >= 0, to < n)
    takes_far = jnp.logical_and(frm >= 0, frm < n)
    to = jnp.clip(to, 0, n - 1)
    frm = jnp.clip(frm, 0, n - 1)
    partner = r + 1 - 2 * parity

    def across(stage):
        width = 1 << stage
        return r + width - 2 * width * ((r // width) % 2)

    load = pltpu.make_async_copy(tiles_hbm, tiles, tile_sem)
    load.start()

    barrier = pltpu.get_barrier_semaphore()
    for stage in range(stages):
        pl.semaphore_signal(barrier, inc=1, device_id={"rows": across(stage)}, device_id_type=MESH)

    @pl.when(sends_far)
    def _():
        pl.semaphore_signal(barrier, inc=1, device_id={"rows": to}, device_id_type=MESH)

    @pl.when(takes_far)
    def _():
        pl.semaphore_signal(barrier, inc=1, device_id={"rows": frm}, device_id_type=MESH)

    for h in range(HALVES):
        sums[h][total] = jnp.zeros((rows, blk), jnp.float32)
        for b in range(blocks):
            x[h, b] = start_ref[h * rows : (h + 1) * rows, b * blk : (b + 1) * blk]
    pl.semaphore_wait(barrier, stages + sends_far.astype(jnp.int32) + takes_far.astype(jnp.int32))
    load.wait()

    def far_copy(k, h, j):
        part = pl.ds(j * per, per)
        return pltpu.make_async_remote_copy(
            src_ref=far_out.at[k, h, part], dst_ref=far_in.at[k, h, part],
            send_sem=far_send.at[k, h, j], recv_sem=far_recv.at[k, h, j],
            device_id={"rows": to}, device_id_type=MESH,
        )

    def near_copy(k, h, j):
        part = pl.ds(j * per, per)
        return pltpu.make_async_remote_copy(
            src_ref=near_out.at[k, h, part], dst_ref=near_in.at[k, h, part],
            send_sem=near_send.at[k, h, j], recv_sem=near_recv.at[k, h, j],
            device_id={"rows": partner}, device_id_type=MESH,
        )

    def gram_copy(which, stage):
        src, dst = (early, early_in) if which == 0 else (late, late_in)
        return pltpu.make_async_remote_copy(
            src_ref=src.at[stage], dst_ref=dst.at[stage],
            send_sem=gram_send.at[which, stage], recv_sem=gram_recv.at[which, stage],
            device_id={"rows": across(stage)}, device_id_type=MESH,
        )

    def compute(k, h):
        place = sums[h]

        def some(i, acc):
            for u in range(UNROLL):
                s = i * UNROLL + u
                code = code_ref[s]
                opens = code & 1
                both = code >> 1
                b = both // total
                product = jnp.dot(
                    x[h, b], tiles[both - b * total], preferred_element_type=jnp.float32
                )
                acc = jnp.where(opens == 1, 0.0, acc) + product
                place[s] = acc
            return acc

        lax.fori_loop(0, total // UNROLL, some, jnp.zeros((rows, blk), jnp.float32))
        for j in range(CHUNKS):
            for c in range(j * per, (j + 1) * per):
                far_out[k, h, c] = place[code_ref[total + c]]

            @pl.when(sends_far)
            def _():
                far_copy(k, h, j).start()

    def relay(k, h):
        place = sums[h]
        for j in range(CHUNKS):
            for c in range(j * per, (j + 1) * per):
                near_out[k, h, c] = place[code_ref[total + blocks + c]]

            @pl.when(takes_far)
            def _():
                far_copy(k, h, j).wait_recv()
                part = pl.ds(j * per, per)
                near_out[k, h, part] += far_in[k, h, part]

            near_copy(k, h, j).start()

    def finish(k, h):
        place = sums[h]
        for j in range(CHUNKS):
            near_copy(k, h, j).wait_recv()
            for c in range(j * per, (j + 1) * per):
                value = (place[code_ref[total + 2 * blocks + c]] + near_in[k, h, c]).astype(jnp.bfloat16)
                x[h, c] = value
                basis_ref[k, h * rows : (h + 1) * rows, c * blk : (c + 1) * blk] = value

    NT = (((1,), (1,)), ((), ()))
    cut = 2 * blk

    def strips(lo, hi, columns):
        parts = [start_ref[:, columns]] if lo == 0 else []
        parts += [basis_ref[k, :, columns] for k in range(max(lo - 1, 0), hi - 1)]
        return parts[0] if len(parts) == 1 else jnp.concatenate(parts, axis=0)

    def early_gram():
        acc = None
        for i in range(blocks * blk // cut):
            w = strips(0, S, slice(i * cut, (i + 1) * cut))
            d = lax.dot_general(w, w, NT, preferred_element_type=jnp.float32)
            acc = d if acc is None else acc + d
        early[0] = acc

    def late_gram():
        panel = HALVES * rows
        acc, own = None, None
        for i in range(blocks * blk // cut):
            columns = slice(i * cut, (i + 1) * cut)
            w = strips(0, S, columns)
            v = strips(S, S + 1, columns)
            d = lax.dot_general(v, w, NT, preferred_element_type=jnp.float32)
            e = lax.dot_general(v, v, NT, preferred_element_type=jnp.float32)
            acc = d if acc is None else acc + d
            own = e if own is None else own + e
        late[0, 0:panel, :] = acc
        late[0, panel : 2 * panel, :] = jnp.zeros_like(acc)
        late[0, panel : 2 * panel, 0:panel] = own

    def join(which, stage):
        src, dst = (early, early_in) if which == 0 else (late, late_in)
        gram_copy(which, stage).wait_recv()
        src[stage + 1] = src[stage] + dst[stage]
        if stage + 1 < stages:
            gram_copy(which, stage + 1).start()

    pending = []
    for k in range(S):
        for h in range(HALVES):
            if k > 0:
                finish(k - 1, h)
            compute(k, h)
        if k == S - 1:
            early_gram()
            gram_copy(0, 0).start()
        for h in range(HALVES):
            relay(k, h)
            if k == S - 1 and h < stages:
                join(0, h)
    for h in range(HALVES):
        finish(S - 1, h)
    late_gram()
    gram_copy(1, 0).start()
    for stage in range(stages):
        if stage >= HALVES:
            join(0, stage)
        join(1, stage)

    panel = HALVES * rows
    scale = 1.0 / (n * blocks * blk)
    w = S * panel
    gram_ref[0, 0:w, 0:w] = early[stages] * scale
    side = late[stages, 0:panel, :] * scale
    gram_ref[0, w : w + panel, 0:w] = side
    gram_ref[0, 0:w, w : w + panel] = side.T
    gram_ref[0, w : w + panel, w : w + panel] = late[stages, panel : 2 * panel, 0:panel] * scale

    for k in range(S):
        for h in range(HALVES):
            for j in range(CHUNKS):
                near_copy(k, h, j).wait_send()

                @pl.when(sends_far)
                def _():
                    far_copy(k, h, j).wait_send()

    for which in range(2):
        for stage in range(stages):
            gram_copy(which, stage).wait_send()


def body(n, start, tiles, cols, counts):
    panel, rows_dev = start.shape
    blocks, slots, blk, _ = tiles.shape
    total = blocks * slots
    rows = panel // HALVES
    stages = n.bit_length() - 1
    code = schedule(cols, counts, n)
    w = S * panel
    vmem = pl.BlockSpec(memory_space=pltpu.VMEM)
    travel = pltpu.VMEM((S, HALVES, blocks, rows, blk), jnp.float32)
    dma = pltpu.SemaphoreType.DMA
    return pl.pallas_call(
        functools.partial(kernel, n, blocks, slots),
        out_shape=(
            jax.ShapeDtypeStruct((S, panel, rows_dev), jnp.bfloat16),
            jax.ShapeDtypeStruct((1, w + panel, w + panel), jnp.float32),
        ),
        in_specs=[vmem, pl.BlockSpec(memory_space=pl.ANY), pl.BlockSpec(memory_space=pltpu.SMEM)],
        out_specs=(vmem, vmem),
        scratch_shapes=[
            pltpu.VMEM((total, blk, blk), jnp.bfloat16),
            pltpu.VMEM((HALVES, blocks, rows, blk), jnp.bfloat16),
            pltpu.VMEM((total + 1, rows, blk), jnp.float32),
            pltpu.VMEM((total + 1, rows, blk), jnp.float32),
            travel, travel, travel, travel,
            pltpu.VMEM((stages + 1, w, w), jnp.float32),
            pltpu.VMEM((stages, w, w), jnp.float32),
            pltpu.VMEM((stages + 1, 2 * panel, w), jnp.float32),
            pltpu.VMEM((stages, 2 * panel, w), jnp.float32),
            dma,
            dma((S, HALVES, CHUNKS)),
            dma((S, HALVES, CHUNKS)),
            dma((S, HALVES, CHUNKS)),
            dma((S, HALVES, CHUNKS)),
            dma((2, stages)),
            dma((2, stages)),
        ],
        compiler_params=pltpu.CompilerParams(
            collective_id=0, has_side_effects=True, vmem_limit_bytes=40 * 1024 * 1024
        ),
    )(start, tiles.reshape(total, blk, blk), code)


def solution(mesh):
    return jax.shard_map(
        functools.partial(body, mesh.shape["rows"]),
        mesh=mesh,
        in_specs=(P("rhs", "rows"), P("rows", None, None, None), P("rows", None), P("rows")),
        out_specs=(P(None, "rhs", "rows"), P("rhs", None, None)),
        check_vma=False,
    )
```

time: 180 us -> 72.1 us (0.40)
  waiting for transfers between devices: 113 us -> 0 us
  Pallas kernels: 0 us -> 64.3 us
  starting transfers between devices: 23.8 us -> 0 us
  matrix products: 22.5 us -> 0 us
  between operations: 14.3 us -> 0.68 us
  local copies, waits for them, and re-layouts: 2.32 us -> 5.24 us
  other arithmetic: 4.06 us -> 1.6 us
    psum x1 -> x0, waiting for transfers between devices: 72.6 us -> none  [body(): gram = lax.psum(local_gram, 'rows')]
    pallas_call x0 -> x1, Pallas kernels: none -> 64.3 us  [body(): pl.pallas_call(functools.partial(kernel, n, blocks, slots), out_shape=(ja...]
    ppermute x8 -> x0, waiting for transfers between devices: 40.4 us -> none  [shifted(): return lax.ppermute(block, axis, route)]
    ppermute x8 -> x0, starting transfers between devices: 23.7 us -> none  [shifted(): return lax.ppermute(block, axis, route)]
    dot_general x13 -> x0, matrix products: 22.5 us -> none  [the longest x4 7.39 us: place_sum(): jnp.einsum('sb,spj->pbj', onehot, remainder, preferred_element_type=jnp.f...]
    unnamed x15 -> x6, local copies, waits for them, and re-layouts: 1.99 us -> 5.15 us
  transfers between devices with their start and end apart: 9 -> 0, of which waited for: 8 -> 0; matrix products, arithmetic and copies ran while one was open for 0% -> 0% of each run, Pallas kernels for 0% -> 0%
where the time goes in v1:
time: 72.1 us; the launch traced here: 71.8 us
  Pallas kernels  64.3 us (89%)
  local copies, waits for them, and re-layouts  5.24 us (7%)
  other arithmetic  1.6 us (2%)
    pallas_call x1, Pallas kernels, body(): pl.pallas_call(functools.partial(kernel, n, blocks, slots), out_shape=(ja...  64.3 us
    unnamed x6, local copies, waits for them, and re-layouts  5.15 us

profile of v1, /device:TPU:0, one launch (start us, length us, event | category | flops | bytes accessed | tf_op | source)
XLA Modules:
  0.0 71.8 jit_solution(12069099165709578317)
XLA Ops:
  0.6 0.8 %fusion.4 = s32[16,12]{1,0:T(8,128)S(1)} fusion(s32[16,12]{1,0:T(8,128)} %param.6, s32[]{:T(128)S(6)} %mul.27, s32[16]{0:T(128)} %param.7, pred[]{:T(512)S(6)} %eq.30), kind=kLoop, calls=%fused_computation.16 | loop fusion | flops 5568 | bytes 1605 | tf_op jit(solution)/shard_map/jit(_where)/select_n | solution.py:27
  1.4 0.1 lt.60
  1.5 0.1 convert_reduce_fusion.1
  1.6 0.1 fusion.2
  1.8 0.2 fusion.1
  1.9 0.2 convert_reduce_fusion
  2.2 0.1 select_reduce_fusion
  2.3 0.1 pad_add_fusion.code_ref
  2.4 0.0 copy-start
  2.4 2.8 %copy-done = bf16[16,12,128,128]{3,2,1,0:T(8,128)(2,1)S(1)} copy-done((bf16[16,12,128,128]{3,2,1,0:T(8,128)(2,1)S(1)}, bf16[16,12,128,128]{3,2,1,0:T(8,128)(2,1)}, u32[]{:S(2)}) %copy-start) | copy-done | bytes 6291480
  5.1 0.0 copy-start.1
  5.2 0.9 %copy-done.1 = bf16[32,2048]{1,0:T(8,128)(2,1)S(1)} copy-done((bf16[32,2048]{1,0:T(8,128)(2,1)S(1)}, bf16[32,2048]{1,0:T(8,128)(2,1)}, u32[]{:S(2)}) %copy-start.1) | copy-done | bytes 131096
  6.1 64.3 %shard_map.59 = (bf16[4,32,2048]{2,1,0:T(8,128)(2,1)S(1)}, f32[1,160,160]{2,1,0:T(8,128)S(1)}) custom-call(bf16[32,2048]{1,0:T(8,128)(2,1)S(1)} %copy-done.1, bf16[192,128,128]{2,1,0:T(8,128)(2,1)S(1)} %bitcast.1, s32[240]{0:T(256)S(1)} %pad_add_fusion.code_ref), custom_call_target="tpu_custom_call" | custom-call | tf_op jit(solution)/shard_map/pallas_call | solution.py:257
  70.4 0.8 %copy.8 = bf16[4,32,2048]{2,1,0:T(8,128)(2,1)} copy(bf16[4,32,2048]{2,1,0:T(8,128)(2,1)S(1)} %get-tuple-element.4) | data formatting | bytes 1048576
  71.2 0.7 copy.9
  (2 shorter events, 0.0 us)
Async XLA Ops:
  2.4 2.8 %copy-start = (bf16[16,12,128,128]{3,2,1,0:T(8,128)(2,1)S(1)}, bf16[16,12,128,128]{3,2,1,0:T(8,128)(2,1)}, u32[]{:S(2)}) copy-start(bf16[16,12,128,128]{3,2,1,0:T(8,128)(2,1)} %param.5) | copy-start | bytes 18874372
  5.1 0.9 %copy-start.1 = (bf16[32,2048]{1,0:T(8,128)(2,1)S(1)}, bf16[32,2048]{1,0:T(8,128)(2,1)}, u32[]{:S(2)}) copy-start(bf16[32,2048]{1,0:T(8,128)(2,1)} %start_ref.1) | copy-start | bytes 393220

commit v2 on v1

v2 whole, which is shorter than its diff:
```python
import functools

import jax
import jax.numpy as jnp
from jax import lax
from jax.experimental import pallas as pl
from jax.experimental.pallas import tpu as pltpu
from jax.sharding import PartitionSpec as P

S = 4
HALVES = 2
CHUNKS = 4
UNROLL = 16
MESH = pl.DeviceIdType.MESH


def schedule(cols, counts, devices):
    blocks, slots = cols.shape
    total = blocks * slots
    r = lax.axis_index("rows")
    rel = cols - (r - 1) * blocks
    side = rel // blocks
    even = r % 2 == 0
    group = jnp.where(side == 1, 2, jnp.where((side == 0) == even, 0, 1))
    target = group * blocks + rel % blocks
    used = jnp.arange(slots, dtype=jnp.int32)[None, :] < counts[:, None]
    target = jnp.where(used, target, 3 * blocks).reshape(-1)
    item = jnp.arange(total, dtype=jnp.int32)
    earlier = target[None, :] < target[:, None]
    tied = (target[None, :] == target[:, None]) & (item[None, :] < item[:, None])
    rank = jnp.sum(earlier | tied, axis=1, dtype=jnp.int32)
    opens = jnp.logical_not(jnp.any(tied, axis=1)).astype(jnp.int32)
    code = item * 2 + opens
    placed = jnp.sum(jnp.where(rank[None, :] == item[:, None], code[None, :], 0), axis=1, dtype=jnp.int32)
    c = jnp.arange(3 * blocks, dtype=jnp.int32)[:, None]
    upto = jnp.sum(target[None, :] <= c, axis=1, dtype=jnp.int32)
    here = jnp.any(target[None, :] == c, axis=1)
    last = jnp.where(here, upto - 1, total)
    return jnp.concatenate([placed, last])


def kernel(
    n, blocks, slots, start_ref, tiles, code_ref, basis_ref, gram_ref,
    products, sums0, sums1, far_out, far_in, near_out, near_in,
    gram0, gram0_in, gram1, gram1_in, gram2, gram2_in,
    far_send, far_recv, near_send, near_recv, gram_send, gram_recv,
):
    total = blocks * slots
    sums = (sums0, sums1)
    grams = ((gram0, gram0_in), (gram1, gram1_in), (gram2, gram2_in))
    rows = start_ref.shape[0] // HALVES
    blk = tiles.shape[-1]
    per = blocks // CHUNKS
    stages = n.bit_length() - 1
    r = lax.axis_index("rows")
    parity = r % 2
    step = 4 * parity - 2
    to, frm = r + step, r - step
    sends_far = jnp.logical_and(to >= 0, to < n)
    takes_far = jnp.logical_and(frm >= 0, frm < n)
    to = jnp.clip(to, 0, n - 1)
    frm = jnp.clip(frm, 0, n - 1)
    partner = r + 1 - 2 * parity

    def across(stage):
        width = 1 << stage
        return r + width - 2 * width * ((r // width) % 2)

    barrier = pltpu.get_barrier_semaphore()
    for stage in range(stages):
        pl.semaphore_signal(barrier, inc=1, device_id={"rows": across(stage)}, device_id_type=MESH)

    @pl.when(sends_far)
    def _():
        pl.semaphore_signal(barrier, inc=1, device_id={"rows": to}, device_id_type=MESH)

    @pl.when(takes_far)
    def _():
        pl.semaphore_signal(barrier, inc=1, device_id={"rows": frm}, device_id_type=MESH)

    for h in range(HALVES):
        sums[h][total] = jnp.zeros((rows, blk), jnp.float32)
    pl.semaphore_wait(barrier, stages + sends_far.astype(jnp.int32) + takes_far.astype(jnp.int32))

    def far_copy(k, h, j):
        part = pl.ds(j * per, per)
        return pltpu.make_async_remote_copy(
            src_ref=far_out.at[k, h, part], dst_ref=far_in.at[k, h, part],
            send_sem=far_send.at[k, h, j], recv_sem=far_recv.at[k, h, j],
            device_id={"rows": to}, device_id_type=MESH,
        )

    def near_copy(k, h, j):
        part = pl.ds(j * per, per)
        return pltpu.make_async_remote_copy(
            src_ref=near_out.at[k, h, part], dst_ref=near_in.at[k, h, part],
            send_sem=near_send.at[k, h, j], recv_sem=near_recv.at[k, h, j],
            device_id={"rows": partner}, device_id_type=MESH,
        )

    def gram_copy(which, stage):
        src, dst = grams[which]
        return pltpu.make_async_remote_copy(
            src_ref=src.at[stage], dst_ref=dst.at[stage],
            send_sem=gram_send.at[which, stage], recv_sem=gram_recv.at[which, stage],
            device_id={"rows": across(stage)}, device_id_type=MESH,
        )

    zero = jnp.zeros((rows, blk), jnp.bfloat16)

    def multiply(pair, upper, lower):
        a, b = 2 * pair * slots, (2 * pair + 1) * slots
        left = jnp.concatenate(
            [jnp.concatenate([upper, zero], axis=1), jnp.concatenate([zero, lower], axis=1)], axis=0
        )
        for t in range(0, slots, 2):
            right = jnp.concatenate(
                [
                    jnp.concatenate([tiles[a + t], tiles[a + t + 1]], axis=1),
                    jnp.concatenate([tiles[b + t], tiles[b + t + 1]], axis=1),
                ],
                axis=0,
            )
            out = jnp.dot(left, right, preferred_element_type=jnp.float32)
            products[a + t] = out[:rows, :blk]
            products[a + t + 1] = out[:rows, blk:]
            products[b + t] = out[rows:, :blk]
            products[b + t + 1] = out[rows:, blk:]

    def advance(k, h):
        for j in range(CHUNKS):
            if k > 0:
                values = finish(k - 1, h, j)
            else:
                values = [
                    start_ref[h * rows : (h + 1) * rows, c * blk : (c + 1) * blk]
                    for c in range(j * per, (j + 1) * per)
                ]
            for p in range(per // 2):
                multiply(j * per // 2 + p, values[2 * p], values[2 * p + 1])

    def collect(k, h):
        place = sums[h]

        def some(i, acc):
            for u in range(UNROLL):
                s = i * UNROLL + u
                code = code_ref[s]
                acc = jnp.where((code & 1) == 1, 0.0, acc) + products[code >> 1]
                place[s] = acc
            return acc

        lax.fori_loop(0, total // UNROLL, some, jnp.zeros((rows, blk), jnp.float32))
        for j in range(CHUNKS):
            for c in range(j * per, (j + 1) * per):
                far_out[k, h, c] = place[code_ref[total + c]]

            @pl.when(sends_far)
            def _():
                far_copy(k, h, j).start()

    def relay(k, h):
        place = sums[h]
        for j in range(CHUNKS):
            for c in range(j * per, (j + 1) * per):
                near_out[k, h, c] = place[code_ref[total + blocks + c]]

            @pl.when(takes_far)
            def _():
                far_copy(k, h, j).wait_recv()
                part = pl.ds(j * per, per)
                near_out[k, h, part] += far_in[k, h, part]

            near_copy(k, h, j).start()

    def finish(k, h, j):
        place = sums[h]
        near_copy(k, h, j).wait_recv()
        values = []
        for c in range(j * per, (j + 1) * per):
            value = (place[code_ref[total + 2 * blocks + c]] + near_in[k, h, c]).astype(jnp.bfloat16)
            basis_ref[k, h * rows : (h + 1) * rows, c * blk : (c + 1) * blk] = value
            values.append(value)
        return values

    NT = (((1,), (1,)), ((), ()))
    panel = HALVES * rows
    cut = 2 * blk

    def strips(lo, hi, columns):
        parts = [start_ref[:, columns]] if lo == 0 else []
        parts += [basis_ref[k, :, columns] for k in range(max(lo - 1, 0), hi - 1)]
        return parts[0] if len(parts) == 1 else jnp.concatenate(parts, axis=0)

    def product(rows_of, columns_of):
        acc = None
        for i in range(blocks * blk // cut):
            columns = slice(i * cut, (i + 1) * cut)
            d = lax.dot_general(
                strips(*rows_of, columns), strips(*columns_of, columns), NT,
                preferred_element_type=jnp.float32,
            )
            acc = d if acc is None else acc + d
        return acc

    def open_gram(which):
        if which == 0:
            gram0[0] = jnp.zeros(gram0.shape[1:], jnp.float32)
            gram0[0, :, 0 : (S - 1) * panel] = product((0, S - 1), (0, S - 1))
        elif which == 1:
            gram1[0] = product((S - 1, S), (0, S))
        else:
            gram2[0, 0:panel] = product((S, S + 1), (0, S))
            gram2[0, panel : 2 * panel, :] = jnp.zeros((panel, S * panel), jnp.float32)
            gram2[0, panel : 2 * panel, 0:panel] = product((S, S + 1), (S, S + 1))
        gram_copy(which, 0).start()

    def join(which, stage):
        src, dst = grams[which]
        gram_copy(which, stage).wait_recv()
        src[stage + 1] = src[stage] + dst[stage]
        if stage + 1 < stages:
            gram_copy(which, stage + 1).start()

    joined = [0, 0, 0]

    def more(which):
        if joined[which] < stages:
            join(which, joined[which])
            joined[which] += 1

    for k in range(S):
        advance(k, 0)
        if k == S - 1:
            more(0)
        collect(k, 0)
        advance(k, 1)
        if k == S - 1:
            open_gram(1)
        relay(k, 0)
        collect(k, 1)
        if k == S - 2:
            open_gram(0)
        relay(k, 1)
        if k == S - 2:
            more(0)
        if k == S - 1:
            more(1)
            more(0)
    for h in range(HALVES):
        for j in range(CHUNKS):
            finish(S - 1, h, j)
        if h == 0:
            more(1)
    open_gram(2)
    for stage in range(stages):
        for which in range(3):
            more(which)

    scale = 1.0 / (n * blocks * blk)
    w = S * panel
    for which, at in ((1, S - 1), (2, S)):
        side = grams[which][0][stages, 0:panel, 0 : at * panel] * scale
        gram_ref[0, at * panel : (at + 1) * panel, 0 : at * panel] = side
        gram_ref[0, 0 : at * panel, at * panel : (at + 1) * panel] = side.T
    v = (S - 1) * panel
    gram_ref[0, 0:v, 0:v] = gram0[stages, :, 0:v] * scale
    gram_ref[0, v:w, v:w] = gram1[stages, :, v:w] * scale
    gram_ref[0, w : w + panel, w : w + panel] = gram2[stages, panel : 2 * panel, 0:panel] * scale

    for k in range(S):
        for h in range(HALVES):
            for j in range(CHUNKS):
                near_copy(k, h, j).wait_send()

                @pl.when(sends_far)
                def _():
                    far_copy(k, h, j).wait_send()

    for which in range(3):
        for stage in range(stages):
            gram_copy(which, stage).wait_send()


def body(n, start, tiles, cols, counts):
    panel, rows_dev = start.shape
    blocks, slots, blk, _ = tiles.shape
    total = blocks * slots
    rows = panel // HALVES
    stages = n.bit_length() - 1
    code = schedule(cols, counts, n)
    w = S * panel
    vmem = pl.BlockSpec(memory_space=pltpu.VMEM)
    travel = pltpu.VMEM((S, HALVES, blocks, rows, blk), jnp.float32)
    dma = pltpu.SemaphoreType.DMA
    return pl.pallas_call(
        functools.partial(kernel, n, blocks, slots),
        out_shape=(
            jax.ShapeDtypeStruct((S, panel, rows_dev), jnp.bfloat16),
            jax.ShapeDtypeStruct((1, w + panel, w + panel), jnp.float32),
        ),
        in_specs=[vmem, vmem, pl.BlockSpec(memory_space=pltpu.SMEM)],
        out_specs=(vmem, vmem),
        scratch_shapes=[
            pltpu.VMEM((total, rows, blk), jnp.float32),
            pltpu.VMEM((total + 1, rows, blk), jnp.float32),
            pltpu.VMEM((total + 1, rows, blk), jnp.float32),
            travel, travel, travel, travel,
            pltpu.VMEM((stages + 1, w - panel, w), jnp.float32),
            pltpu.VMEM((stages, w - panel, w), jnp.float32),
            pltpu.VMEM((stages + 1, panel, w), jnp.float32),
            pltpu.VMEM((stages, panel, w), jnp.float32),
            pltpu.VMEM((stages + 1, 2 * panel, w), jnp.float32),
            pltpu.VMEM((stages, 2 * panel, w), jnp.float32),
            dma((S, HALVES, CHUNKS)),
            dma((S, HALVES, CHUNKS)),
            dma((S, HALVES, CHUNKS)),
            dma((S, HALVES, CHUNKS)),
            dma((3, stages)),
            dma((3, stages)),
        ],
        compiler_params=pltpu.CompilerParams(
            collective_id=0, has_side_effects=True, vmem_limit_bytes=40 * 1024 * 1024
        ),
    )(start, tiles.reshape(total, blk, blk), code)


def solution(mesh):
    return jax.shard_map(
        functools.partial(body, mesh.shape["rows"]),
        mesh=mesh,
        in_specs=(P("rhs", "rows"), P("rows", None, None, None), P("rows", None), P("rows")),
        out_specs=(P(None, "rhs", "rows"), P("rhs", None, None)),
        check_vma=False,
    )
```

time: 72.1 us -> 69.5 us (0.964)
  Pallas kernels: 64.3 us -> 61.8 us
    pallas_call x1, Pallas kernels: 64.3 us -> 61.8 us  [body(): pl.pallas_call(functools.partial(kernel, n, blocks, slots), out_shape=(ja...]
where the time goes in v2:
time: 69.5 us; the launch traced here: 69.3 us
  Pallas kernels  61.8 us (89%)
  local copies, waits for them, and re-layouts  5.24 us (8%)
  other arithmetic  1.59 us (2%)
    pallas_call x1, Pallas kernels, body(): pl.pallas_call(functools.partial(kernel, n, blocks, slots), out_shape=(ja...  61.8 us
    unnamed x6, local copies, waits for them, and re-layouts  5.15 us

profile of v2, /device:TPU:0, one launch (start us, length us, event | category | flops | bytes accessed | tf_op | source)
XLA Modules:
  0.0 69.3 jit_solution(14120167402956490623)
XLA Ops:
  0.6 0.8 %fusion.4 = s32[16,12]{1,0:T(8,128)S(1)} fusion(s32[16,12]{1,0:T(8,128)} %param.6, s32[]{:T(128)S(6)} %mul.17, s32[16]{0:T(128)} %param.7, pred[]{:T(512)S(6)} %eq.30), kind=kLoop, calls=%fused_computation.16 | loop fusion | flops 5568 | bytes 1605 | tf_op jit(solution)/shard_map/jit(_where)/select_n | solution.py:27
  1.4 0.1 lt.60
  1.5 0.1 convert_reduce_fusion.1
  1.6 0.1 fusion.2
  1.8 0.2 fusion.1
  1.9 0.2 convert_reduce_fusion
  2.2 0.1 select_reduce_fusion
  2.3 0.1 pad_add_fusion.code_ref
  2.4 0.0 copy-start
  2.4 2.8 %copy-done = bf16[16,12,128,128]{3,2,1,0:T(8,128)(2,1)S(1)} copy-done((bf16[16,12,128,128]{3,2,1,0:T(8,128)(2,1)S(1)}, bf16[16,12,128,128]{3,2,1,0:T(8,128)(2,1)}, u32[]{:S(2)}) %copy-start) | copy-done | bytes 6291480
  5.1 0.0 copy-start.1
  5.1 0.9 %copy-done.1 = bf16[32,2048]{1,0:T(8,128)(2,1)S(1)} copy-done((bf16[32,2048]{1,0:T(8,128)(2,1)S(1)}, bf16[32,2048]{1,0:T(8,128)(2,1)}, u32[]{:S(2)}) %copy-start.1) | copy-done | bytes 131096
  6.0 61.8 %shard_map.59 = (bf16[4,32,2048]{2,1,0:T(8,128)(2,1)S(1)}, f32[1,160,160]{2,1,0:T(8,128)S(1)}) custom-call(bf16[32,2048]{1,0:T(8,128)(2,1)S(1)} %copy-done.1, bf16[192,128,128]{2,1,0:T(8,128)(2,1)S(1)} %bitcast.1, s32[240]{0:T(256)S(1)} %pad_add_fusion.code_ref), custom_call_target="tpu_custom_call" | custom-call | tf_op jit(solution)/shard_map/pallas_call | solution.py:296
  67.8 0.8 %copy.8 = bf16[4,32,2048]{2,1,0:T(8,128)(2,1)} copy(bf16[4,32,2048]{2,1,0:T(8,128)(2,1)S(1)} %get-tuple-element.4) | data formatting | bytes 1048576
  68.6 0.7 copy.9
  (2 shorter events, 0.0 us)
Async XLA Ops:
  2.4 2.8 %copy-start = (bf16[16,12,128,128]{3,2,1,0:T(8,128)(2,1)S(1)}, bf16[16,12,128,128]{3,2,1,0:T(8,128)(2,1)}, u32[]{:S(2)}) copy-start(bf16[16,12,128,128]{3,2,1,0:T(8,128)(2,1)} %param.5) | copy-start | bytes 18874372
  5.1 0.9 %copy-start.1 = (bf16[32,2048]{1,0:T(8,128)(2,1)S(1)}, bf16[32,2048]{1,0:T(8,128)(2,1)}, u32[]{:S(2)}) copy-start(bf16[32,2048]{1,0:T(8,128)(2,1)} %start_ref.1) | copy-start | bytes 393220

commit v3 on v2

--- a/solution.py
+++ b/solution.py
@@ -40,10 +40,10 @@
 
 
 def kernel(
-    n, blocks, slots, start_ref, tiles, code_ref, basis_ref, gram_ref,
-    products, sums0, sums1, far_out, far_in, near_out, near_in,
+    n, blocks, slots, start_ref, tiles_hbm, code_ref, basis_ref, gram_ref,
+    tiles, products, sums0, sums1, far_out, far_in, near_out, near_in,
     gram0, gram0_in, gram1, gram1_in, gram2, gram2_in,
-    far_send, far_recv, near_send, near_recv, gram_send, gram_recv,
+    tile_sem, far_send, far_recv, near_send, near_recv, gram_send, gram_recv,
 ):
     total = blocks * slots
     sums = (sums0, sums1)
@@ -66,6 +66,13 @@
         width = 1 << stage
         return r + width - 2 * width * ((r // width) % 2)
 
+    def load(j):
+        part = pl.ds(j * per * slots, per * slots)
+        return pltpu.make_async_copy(tiles_hbm.at[part], tiles.at[part], tile_sem.at[j])
+
+    for j in range(CHUNKS):
+        load(j).start()
+
     barrier = pltpu.get_barrier_semaphore()
     for stage in range(stages):
         pl.semaphore_signal(barrier, inc=1, device_id={"rows": across(stage)}, device_id_type=MESH)
@@ -127,17 +134,18 @@
             products[b + t] = out[rows:, :blk]
             products[b + t + 1] = out[rows:, blk:]
 
-    def advance(k, h):
-        for j in range(CHUNKS):
-            if k > 0:
-                values = finish(k - 1, h, j)
-            else:
-                values = [
-                    start_ref[h * rows : (h + 1) * rows, c * blk : (c + 1) * blk]
-                    for c in range(j * per, (j + 1) * per)
-                ]
-            for p in range(per // 2):
-                multiply(j * per // 2 + p, values[2 * p], values[2 * p + 1])
+    def advance(k, h, j):
+        if k > 0:
+            values = finish(k - 1, h, j)
+        else:
+            if h == 0:
+                load(j).wait()
+            values = [
+                start_ref[h * rows : (h + 1) * rows, c * blk : (c + 1) * blk]
+                for c in range(j * per, (j + 1) * per)
+            ]
+        for p in range(per // 2):
+            multiply(j * per // 2 + p, values[2 * p], values[2 * p + 1])
 
     def collect(k, h):
         place = sums[h]
@@ -159,19 +167,18 @@
             def _():
                 far_copy(k, h, j).start()
 
-    def relay(k, h):
+    def relay(k, h, j):
         place = sums[h]
-        for j in range(CHUNKS):
-            for c in range(j * per, (j + 1) * per):
-                near_out[k, h, c] = place[code_ref[total + blocks + c]]
-
-            @pl.when(takes_far)
-            def _():
-                far_copy(k, h, j).wait_recv()
-                part = pl.ds(j * per, per)
-                near_out[k, h, part] += far_in[k, h, part]
-
-            near_copy(k, h, j).start()
+        for c in range(j * per, (j + 1) * per):
+            near_out[k, h, c] = place[code_ref[total + blocks + c]]
+
+        @pl.when(takes_far)
+        def _():
+            far_copy(k, h, j).wait_recv()
+            part = pl.ds(j * per, per)
+            near_out[k, h, part] += far_in[k, h, part]
+
+        near_copy(k, h, j).start()
 
     def finish(k, h, j):
         place = sums[h]
@@ -203,16 +210,28 @@
             acc = d if acc is None else acc + d
         return acc
 
+    def triangle(at, to):
+        place = at * (at + 1) // 2 + to
+        return place // S * panel, place % S * panel
+
     def open_gram(which):
         if which == 0:
+            g = product((0, S - 1), (0, S - 1))
             gram0[0] = jnp.zeros(gram0.shape[1:], jnp.float32)
-            gram0[0, :, 0 : (S - 1) * panel] = product((0, S - 1), (0, S - 1))
+            for at in range(S - 1):
+                for to in range(at + 1):
+                    row, lane = triangle(at, to)
+                    gram0[0, row : row + panel, lane : lane + panel] = g[
+                        at * panel : (at + 1) * panel, to * panel : (to + 1) * panel
+                    ]
         elif which == 1:
             gram1[0] = product((S - 1, S), (0, S))
         else:
             gram2[0, 0:panel] = product((S, S + 1), (0, S))
-            gram2[0, panel : 2 * panel, :] = jnp.zeros((panel, S * panel), jnp.float32)
-            gram2[0, panel : 2 * panel, 0:panel] = product((S, S + 1), (S, S + 1))
+            own = product((S, S + 1), (S, S + 1))
+            gram2[0, panel : panel + panel // S] = jnp.concatenate(
+                [own[q * panel // S : (q + 1) * panel // S] for q in range(S)], axis=1
+            )
         gram_copy(which, 0).start()
 
     def join(which, stage):
@@ -230,28 +249,31 @@
             joined[which] += 1
 
     for k in range(S):
-        advance(k, 0)
+        for j in range(CHUNKS):
+            advance(k, 0, j)
+            if k > 0:
+                relay(k - 1, 1, j)
+        collect(k, 0)
         if k == S - 1:
             more(0)
-        collect(k, 0)
-        advance(k, 1)
+        for j in range(CHUNKS):
+            advance(k, 1, j)
+        relay(k, 0, 0)
+        collect(k, 1)
+        for j in range(1, CHUNKS):
+            relay(k, 0, j)
+        if k >= S - 2:
+            open_gram(k - (S - 2))
         if k == S - 1:
-            open_gram(1)
-        relay(k, 0)
-        collect(k, 1)
-        if k == S - 2:
-            open_gram(0)
-        relay(k, 1)
-        if k == S - 2:
             more(0)
-        if k == S - 1:
-            more(1)
-            more(0)
-    for h in range(HALVES):
-        for j in range(CHUNKS):
-            finish(S - 1, h, j)
-        if h == 0:
-            more(1)
+    for j in range(CHUNKS):
+        finish(S - 1, 0, j)
+        relay(S - 1, 1, j)
+    more(1)
+    more(0)
+    for j in range(CHUNKS):
+        finish(S - 1, 1, j)
+    more(1)
     open_gram(2)
     for stage in range(stages):
         for which in range(3):
@@ -264,9 +286,18 @@
         gram_ref[0, at * panel : (at + 1) * panel, 0 : at * panel] = side
         gram_ref[0, 0 : at * panel, at * panel : (at + 1) * panel] = side.T
     v = (S - 1) * panel
-    gram_ref[0, 0:v, 0:v] = gram0[stages, :, 0:v] * scale
+    for at in range(S - 1):
+        for to in range(at + 1):
+            row, lane = triangle(at, to)
+            block = gram0[stages, row : row + panel, lane : lane + panel] * scale
+            gram_ref[0, at * panel : (at + 1) * panel, to * panel : (to + 1) * panel] = block
+            if to < at:
+                gram_ref[0, to * panel : (to + 1) * panel, at * panel : (at + 1) * panel] = block.T
     gram_ref[0, v:w, v:w] = gram1[stages, :, v:w] * scale
-    gram_ref[0, w : w + panel, w : w + panel] = gram2[stages, panel : 2 * panel, 0:panel] * scale
+    for q in range(S):
+        gram_ref[0, w + q * panel // S : w + (q + 1) * panel // S, w : w + panel] = (
+            gram2[stages, panel : panel + panel // S, q * panel : (q + 1) * panel] * scale
+        )
 
     for k in range(S):
         for h in range(HALVES):
@@ -290,6 +321,7 @@
     stages = n.bit_length() - 1
     code = schedule(cols, counts, n)
     w = S * panel
+    first = -(-(S * (S - 1) // 2) // S)
     vmem = pl.BlockSpec(memory_space=pltpu.VMEM)
     travel = pltpu.VMEM((S, HALVES, blocks, rows, blk), jnp.float32)
     dma = pltpu.SemaphoreType.DMA
@@ -299,19 +331,21 @@
             jax.ShapeDtypeStruct((S, panel, rows_dev), jnp.bfloat16),
             jax.ShapeDtypeStruct((1, w + panel, w + panel), jnp.float32),
         ),
-        in_specs=[vmem, vmem, pl.BlockSpec(memory_space=pltpu.SMEM)],
+        in_specs=[vmem, pl.BlockSpec(memory_space=pl.ANY), pl.BlockSpec(memory_space=pltpu.SMEM)],
         out_specs=(vmem, vmem),
         scratch_shapes=[
+            pltpu.VMEM((total, blk, blk), jnp.bfloat16),
             pltpu.VMEM((total, rows, blk), jnp.float32),
             pltpu.VMEM((total + 1, rows, blk), jnp.float32),
             pltpu.VMEM((total + 1, rows, blk), jnp.float32),
             travel, travel, travel, travel,
-            pltpu.VMEM((stages + 1, w - panel, w), jnp.float32),
-            pltpu.VMEM((stages, w - panel, w), jnp.float32),
+            pltpu.VMEM((stages + 1, first * panel, w), jnp.float32),
+            pltpu.VMEM((stages, first * panel, w), jnp.float32),
             pltpu.VMEM((stages + 1, panel, w), jnp.float32),
             pltpu.VMEM((stages, panel, w), jnp.float32),
-            pltpu.VMEM((stages + 1, 2 * panel, w), jnp.float32),
-            pltpu.VMEM((stages, 2 * panel, w), jnp.float32),
+            pltpu.VMEM((stages + 1, panel + panel // S, w), jnp.float32),
+            pltpu.VMEM((stages, panel + panel // S, w), jnp.float32),
+            dma((CHUNKS,)),
             dma((S, HALVES, CHUNKS)),
             dma((S, HALVES, CHUNKS)),
             dma((S, HALVES, CHUNKS)),
@@ -320,7 +354,7 @@
             dma((3, stages)),
         ],
         compiler_params=pltpu.CompilerParams(
-            collective_id=0, has_side_effects=True, vmem_limit_bytes=40 * 1024 * 1024
+            collective_id=0, has_side_effects=True, vmem_limit_bytes=60 * 1024 * 1024
         ),
     )(start, tiles.reshape(total, blk, blk), code)
 

time: 69.5 us -> 64.4 us (0.927)
  Pallas kernels: 61.8 us -> 57.7 us
  local copies, waits for them, and re-layouts: 5.24 us -> 3.56 us
    pallas_call x1, Pallas kernels: 61.8 us -> 57.7 us  [body(): pl.pallas_call(functools.partial(kernel, n, blocks, slots), out_shape=(ja...]
    unnamed x6 -> x2, local copies, waits for them, and re-layouts: 5.15 us -> 3.47 us
where the time goes in v3:
time: 64.4 us; the launch traced here: 64.1 us
  Pallas kernels  57.7 us (90%)
  local copies, waits for them, and re-layouts  3.56 us (6%)
  other arithmetic  2.16 us (3%)
  between operations  0.68 us (1%)
    pallas_call x1, Pallas kernels, body(): pl.pallas_call(functools.partial(kernel, n, blocks, slots), out_shape=(ja...  57.7 us
    unnamed x2, local copies, waits for them, and re-layouts  3.47 us

profile of v3, /device:TPU:0, one launch (start us, length us, event | category | flops | bytes accessed | tf_op | source)
XLA Modules:
  0.0 64.1 jit_solution(17777385205026439893)
XLA Ops:
  0.6 0.8 %fusion.4 = s32[16,12]{1,0:T(8,128)S(1)} fusion(s32[16,12]{1,0:T(8,128)} %param.6, s32[]{:T(128)S(6)} %mul.17, s32[16]{0:T(128)} %param.7, pred[]{:T(512)S(6)} %eq.30), kind=kLoop, calls=%fused_computation.16 | loop fusion | flops 5568 | bytes 1605 | tf_op jit(solution)/shard_map/jit(_where)/select_n | solution.py:27
  1.4 0.1 lt.60
  1.5 0.1 convert_reduce_fusion.1
  1.6 0.1 fusion.2
  1.8 0.2 fusion.1
  1.9 0.2 convert_reduce_fusion
  2.2 0.1 select_reduce_fusion
  2.3 0.6 %pad_add_fusion.code_ref = s32[240]{0:T(256)} fusion(s32[48]{0:T(128)S(1)} %add_select_fusion.2, s32[192]{0:T(256)S(1)} %select_reduce_fusion), kind=kLoop, calls=%fused_computation.22 | loop fusion | flops 240 | bytes 1920 | tf_op jit(solution)/shard_map/concatenate | solution.py:39
  2.9 57.7 %shard_map.59 = (bf16[4,32,2048]{2,1,0:T(8,128)(2,1)}, f32[1,160,160]{2,1,0:T(8,128)}) custom-call(bf16[32,2048]{1,0:T(8,128)(2,1)} %start_ref.1, bf16[192,128,128]{2,1,0:T(8,128)(2,1)} %bitcast.1, s32[240]{0:T(256)} %pad_add_fusion.code_ref), custom_call_target="tpu_custom_call" | custom-call | tf_op jit(solution)/shard_map/pallas_call | solution.py:328
  60.7 1.9 %copy.8 = bf16[4,32,2048]{2,1,0:T(8,128)(2,1)} copy(bf16[4,32,2048]{2,1,0:T(8,128)(2,1)} %get-tuple-element.4) | data formatting | bytes 1048576
  62.5 1.6 %copy.9 = f32[1,160,160]{2,1,0:T(8,128)} copy(f32[1,160,160]{2,1,0:T(8,128)} %get-tuple-element.5) | data formatting | bytes 204800
  (2 shorter events, 0.0 us)
